TPU v7x, 256 devices: a whole 4x4x8 slice. The times are simulated.
256 devices in a mesh: seq: 64 (over x, z, core), chan: 4 (over y).
Axes of the slice: x: 4, y: 4, z: 8, core: 2. Of those that a mesh axis runs over, the one named last changes fastest.
Arguments:
- q_gate: bfloat16 [32768, 1024], P('seq', 'chan'), may hold values from -6 to 6
- k_gate: bfloat16 [32768, 1024], P('seq', 'chan'), may hold values from -6 to 6
- value: bfloat16 [32768, 1024], P('seq', 'chan'), may hold values from -6 to 6
- decay: float32 [16, 1024], P(None, 'chan'), may hold values from 7.6293945e-06 to 0.0333333333
- residue: float32 [16, 1024], P(None, 'chan'), may hold values from -1 to 1
- skip: float32 [1024], P('chan'), may hold values from -1 to 1
- out_weight: bfloat16 [1024, 1024], P(None, 'chan'), may hold values from -0.1875 to 0.1875
- out_bias: float32 [1024], P('chan'), may hold values from -3 to 3
Outputs:
- layer_out: bfloat16 [32768, 1024], P('seq', 'chan')
All inputs are finite; a program needn't handle non-finite values.
Results may differ from a plain program's by a relative error of at most 0.015.
Values may be sent and summed in bfloat16 or wider, within the bound.
A program may use at most 64 MiB of HBM per device.

v0:
```python
import functools

import jax
import jax.numpy as jnp
from jax import lax
from jax.experimental import pallas as pl
from jax.experimental.pallas import tpu as pltpu
from jax.sharding import PartitionSpec as P

MESH = pl.DeviceIdType.MESH
F32 = jnp.float32
BF16 = jnp.bfloat16
NX, NZ, NC, NY = 4, 8, 2, 4
SUB = 8
LANES = 128
CHUNKS = 4


def rows_of(array, n, lane):
    return jnp.broadcast_to(array[n : n + 1, lane : lane + LANES], (SUB, LANES))


def kernel(
    q_hbm, k_hbm, v_hbm, decay_ref, residue_ref, skip_ref, w_hbm, bias_ref, out_ref,
    k_buf, v_buf, q_buf, w_buf, u_buf, qf_buf, y_buf, h_buf, lam_buf, sub_buf, g_buf,
    z_buf, x_buf, mate_s, mate_pre, t_buf, p_buf, gathered, o_buf,
    load_sem, z_send, z_recv, x_send, x_recv, mate_send, mate_recv, y_send, y_recv,
):
    modes, channels = decay_ref.shape
    tokens = u_buf.shape[1]
    steps = tokens // SUB
    part = steps // CHUNKS
    lane_starts = range(0, channels, LANES)
    seq = lax.axis_index("seq")
    y = lax.axis_index("chan")
    x, z, core = seq // (NZ * NC), (seq // NC) % NZ, seq % NC

    def device(xx, zz, cc, yy):
        return ((xx * NZ + zz) * NC + cc, yy)

    loads = [
        pltpu.make_async_copy(src, dst, load_sem.at[i])
        for i, (src, dst) in enumerate(
            [(k_hbm, k_buf), (v_hbm, v_buf), (q_hbm, q_buf), (w_hbm, w_buf)]
        )
    ]
    for load in loads:
        load.start()

    x_buf[...] = jnp.zeros_like(x_buf)
    barrier = pltpu.get_barrier_semaphore()
    partners = [device(x, z, 1 - core, y)]
    z_order = (4, 3, 5, 2, 6, 1, 7)
    partners += [device(x, (z + k) % NZ, core, y) for k in z_order]
    partners += [device((x + k) % NX, z, cc, y) for k in range(1, NX) for cc in range(NC)]
    partners += [device(x, z, core, (y + k) % NY) for k in range(1, NY)]
    for partner in partners:
        pl.semaphore_signal(barrier, inc=1, device_id=partner, device_id_type=MESH)

    decay = decay_ref[...]
    lam_buf[...] = jnp.exp(-decay)

    loads[0].wait()
    loads[1].wait()
    for lane in lane_starts:
        k_part, v_part = (buf[:, pl.ds(lane, LANES)].astype(F32) for buf in (k_buf, v_buf))
        u_buf[lane // LANES] = (k_part * v_part).astype(BF16).astype(F32)

    sublane = lax.broadcasted_iota(jnp.int32, (SUB, LANES), 0)
    for lane in lane_starts:
        lam = [rows_of(lam_buf[...], n, lane) for n in range(modes)]

        def advance(b, state, lam=lam, lane=lane):
            u = u_buf[lane // LANES, pl.ds(b, SUB, stride=steps), :]
            return tuple(l * h + u for l, h in zip(lam, state))

        zero = jnp.zeros((SUB, LANES), F32)
        state = lax.fori_loop(0, steps, advance, (zero,) * modes, unroll=8)
        for n in range(modes):
            run = state[n]
            for shift in (1, 2, 4):
                factor = jnp.exp(-rows_of(decay, n, lane) * float(steps * shift))
                moved = jnp.where(sublane >= shift, pltpu.roll(run, shift, 0), 0.0)
                run = run + factor * moved
            z_buf[pl.ds(z, 1), pl.ds(n, 1), pl.ds(lane, LANES)] = run[SUB - 1 : SUB].reshape(1, 1, LANES)
            h_buf[n, :, pl.ds(lane, LANES)] = jnp.where(sublane >= 1, pltpu.roll(run, 1, 0), 0.0)

    pl.semaphore_wait(barrier, len(partners))

    z_copies = [
        pltpu.make_async_remote_copy(
            src_ref=z_buf.at[z], dst_ref=z_buf.at[z],
            send_sem=z_send.at[i], recv_sem=z_recv.at[z],
            device_id=device(x, (z + k) % NZ, core, y), device_id_type=MESH,
        )
        for i, k in enumerate(z_order)
    ]
    for copy in z_copies:
        copy.start()
    mate = device(x, z, 1 - core, y)
    s_copy = pltpu.make_async_remote_copy(
        src_ref=z_buf.at[z], dst_ref=mate_s, send_sem=mate_send.at[0], recv_sem=mate_recv.at[0],
        device_id=mate, device_id_type=MESH,
    )
    s_copy.start()

    for lane in lane_starts:
        lam = [rows_of(lam_buf[...], n, lane) for n in range(modes)]
        weight = [rows_of(residue_ref[...], n, lane) for n in range(modes)]
        skip_row = jnp.broadcast_to(skip_ref[:, lane : lane + LANES], (SUB, LANES))

        def local(b, state, lam=lam, weight=weight, skip_row=skip_row, lane=lane):
            u = u_buf[lane // LANES, pl.ds(b, SUB, stride=steps), :]
            state = tuple(l * h + u for l, h in zip(lam, state))
            total = [w * h for w, h in zip(weight, state)] + [skip_row * u]
            while len(total) > 1:
                total = [a + c for a, c in zip(total[::2], total[1::2])] + total[len(total) // 2 * 2 :]
            y_buf[b, :, pl.ds(lane, LANES)] = total[0]
            return state

        first = tuple(h_buf[n, :, pl.ds(lane, LANES)] for n in range(modes))
        lax.fori_loop(0, steps, local, first, unroll=2)
        for n in range(modes):
            place = (sublane * steps + 1).astype(F32)
            sub_buf[n, :, pl.ds(lane, LANES)] = weight[n] * jnp.exp(-rows_of(decay, n, lane) * place)
    loads[2].wait()
    for lane in lane_starts:
        qf_buf[lane // LANES] = q_buf[:, pl.ds(lane, LANES)].astype(F32)

    chip_power = jnp.exp(-decay * float(NC * tokens))
    row_power = jnp.exp(-decay * float(NZ * NC * tokens))
    half_power = jnp.exp(-decay * float(tokens))
    place_power = jnp.exp(-decay * (z * (NC * tokens)).astype(F32))

    for copy in z_copies:
        copy.wait_send()
    for k in range(1, NZ):
        src = (z + k) % NZ
        pltpu.make_async_remote_copy(
            src_ref=z_buf.at[src], dst_ref=z_buf.at[src], send_sem=z_send.at[0],
            recv_sem=z_recv.at[src], device_id=mate, device_id_type=MESH,
        ).wait_recv()
    total = jnp.zeros_like(decay)
    prefix = jnp.zeros_like(decay)
    for zz in range(NZ):
        prefix = jnp.where(z == zz, total, prefix)
        total = chip_power * total + z_buf[zz]
    t_buf[...] = total
    p_buf[...] = prefix

    for k in range(1, NX):
        @pl.when(x + k < NX)
        def _(k=k):
            for cc in range(NC):
                pltpu.make_async_remote_copy(
                    src_ref=t_buf, dst_ref=x_buf.at[core, x],
                    send_sem=x_send.at[k - 1, cc], recv_sem=x_recv.at[core, x],
                    device_id=device(x + k, z, cc, y), device_id_type=MESH,
                ).start()
    p_copy = pltpu.make_async_remote_copy(
        src_ref=p_buf, dst_ref=mate_pre, send_sem=mate_send.at[1], recv_sem=mate_recv.at[1],
        device_id=mate, device_id_type=MESH,
    )
    p_copy.start()
    s_copy.wait()
    p_copy.wait()
    for k in range(1, NX):
        @pl.when(x >= k)
        def _(k=k):
            for cc in range(NC):
                pltpu.make_async_remote_copy(
                    src_ref=t_buf, dst_ref=x_buf.at[cc, x - k],
                    send_sem=x_send.at[0, 0], recv_sem=x_recv.at[cc, x - k],
                    device_id=mate, device_id_type=MESH,
                ).wait_recv()

    before = jnp.zeros_like(decay)
    for xx in range(NX - 1):
        step = half_power * x_buf[0, xx] + x_buf[1, xx]
        before = jnp.where(xx < x, row_power * before + step, before)
    other = mate_pre[...]
    early = jnp.where(core == 0, prefix, other)
    late = jnp.where(core == 0, other, prefix)
    carry = place_power * before + half_power * early + late
    carry = jnp.where(core == 0, carry, half_power * carry + mate_s[...])
    g_buf[...] = carry

    y_copies = []
    for lane in lane_starts:
        for n in range(modes):
            h_buf[n, :, pl.ds(lane, LANES)] = sub_buf[n, :, pl.ds(lane, LANES)] * rows_of(g_buf[...], n, lane)
    for j in range(CHUNKS):
        for lane in lane_starts:
            lam = [rows_of(lam_buf[...], n, lane) for n in range(modes)]

            def finish(i, state, lam=lam, lane=lane, j=j):
                pair = []
                for o in range(2):
                    b = j * part + 2 * i + o
                    total = list(state) + [y_buf[b, :, pl.ds(lane, LANES)]]
                    while len(total) > 1:
                        total = [a + c for a, c in zip(total[::2], total[1::2])] + total[len(total) // 2 * 2 :]
                    gate = qf_buf[lane // LANES, pl.ds(b, SUB, stride=steps), :]
                    pair.append(gate * total[0])
                    state = tuple(l * h for l, h in zip(lam, state))
                rows = jnp.concatenate(pair, axis=0).astype(BF16)
                start = pl.multiple_of(i * 2 * SUB, 2 * SUB)
                gathered[y, j, pl.ds(start, 2 * SUB), pl.ds(lane, LANES)] = rows
                return state

            first = tuple(h_buf[n, :, pl.ds(lane, LANES)] for n in range(modes))
            last = lax.fori_loop(0, part // 2, finish, first)
            for n in range(modes):
                h_buf[n, :, pl.ds(lane, LANES)] = last[n]
        for i, k in enumerate((2, 1, 3)):
            copy = pltpu.make_async_remote_copy(
                src_ref=gathered.at[y, j], dst_ref=gathered.at[y, j],
                send_sem=y_send.at[i, j], recv_sem=y_recv.at[y, j],
                device_id=device(x, z, core, (y + k) % NY), device_id_type=MESH,
            )
            copy.start()
            y_copies.append(copy)

    loads[3].wait()
    bias = jnp.broadcast_to(bias_ref[...], (part * SUB, channels))
    for j in range(CHUNKS):
        for k in range(1, NY):
            src = (y + k) % NY
            pltpu.make_async_remote_copy(
                src_ref=gathered.at[src, j], dst_ref=gathered.at[src, j],
                send_sem=y_send.at[0, 0], recv_sem=y_recv.at[src, j],
                device_id=mate, device_id_type=MESH,
            ).wait_recv()
        projected = bias
        for yy in range(NY):
            projected = projected + jnp.dot(
                gathered[yy, j], w_buf[pl.ds(yy * channels, channels), :], preferred_element_type=F32
            )
        for i in range(part):
            for lane in lane_starts:
                o_buf[lane // LANES, pl.ds(j * part + i, SUB, stride=steps), :] = projected[
                    i * SUB : (i + 1) * SUB, lane : lane + LANES
                ]
    for lane in lane_starts:
        out_ref[:, pl.ds(lane, LANES)] = o_buf[lane // LANES].astype(BF16)

    for copy in y_copies:
        copy.wait_send()
    for k in range(1, NX):
        @pl.when(x + k < NX)
        def _(k=k):
            for cc in range(NC):
                pltpu.make_async_remote_copy(
                    src_ref=t_buf, dst_ref=x_buf.at[core, x],
                    send_sem=x_send.at[k - 1, cc], recv_sem=x_recv.at[core, x],
                    device_id=device(x + k, z, cc, y), device_id_type=MESH,
                ).wait_send()


def layer(q_gate, k_gate, value, decay, residue, skip, out_weight, out_bias):
    tokens, channels = q_gate.shape
    modes = decay.shape[0]
    part_rows = tokens // CHUNKS
    dma = pltpu.SemaphoreType.DMA
    state = (modes, channels)
    any_spec = pl.BlockSpec(memory_space=pl.ANY)
    vmem = pl.BlockSpec(memory_space=pltpu.VMEM)
    return pl.pallas_call(
        kernel,
        out_shape=jax.ShapeDtypeStruct((tokens, channels), BF16),
        in_specs=[any_spec, any_spec, any_spec, vmem, vmem, vmem, any_spec, vmem],
        out_specs=vmem,
        scratch_shapes=[
            pltpu.VMEM((tokens, channels), BF16),
            pltpu.VMEM((tokens, channels), BF16),
            pltpu.VMEM((tokens, channels), BF16),
            pltpu.VMEM(out_weight.shape, BF16),
            pltpu.VMEM((channels // LANES, tokens, LANES), F32),
            pltpu.VMEM((channels // LANES, tokens, LANES), F32),
            pltpu.VMEM((tokens // SUB, SUB, channels), F32),
            pltpu.VMEM((modes, SUB, channels), F32),
            pltpu.VMEM(state, F32),
            pltpu.VMEM((modes, SUB, channels), F32),
            pltpu.VMEM(state, F32),
            pltpu.VMEM((NZ,) + state, F32),
            pltpu.VMEM((NC, NX) + state, F32),
            pltpu.VMEM(state, F32),
            pltpu.VMEM(state, F32),
            pltpu.VMEM(state, F32),
            pltpu.VMEM(state, F32),
            pltpu.VMEM((NY, CHUNKS, part_rows, channels), BF16),
            pltpu.VMEM((channels // LANES, tokens, LANES), F32),
            dma((4,)), dma((NZ - 1,)), dma((NZ,)), dma((NX - 1, NC)), dma((NC, NX)),
            dma((2,)), dma((2,)), dma((NY - 1, CHUNKS)), dma((NY, CHUNKS)),
        ],
        compiler_params=pltpu.CompilerParams(
            collective_id=0, has_side_effects=True, vmem_limit_bytes=32 * 2**20
        ),
        name="layer",
    )(q_gate, k_gate, value, decay, residue, skip.reshape(1, -1), out_weight, out_bias.reshape(1, -1))


def solution(mesh):
    return jax.shard_map(
        layer,
        mesh=mesh,
        in_specs=(
            P("seq", "chan"),
            P("seq", "chan"),
            P("seq", "chan"),
            P(None, "chan"),
            P(None, "chan"),
            P("chan"),
            P(None, "chan"),
            P("chan"),
        ),
        out_specs=P("seq", "chan"),
        check_vma=False,
    )
```

profile of v0, /device:TPU:6, one launch (start us, length us, event | category | flops | bytes accessed | tf_op | source)
XLA Modules:
  0.0 38.8 jit_solution(11714583018961114902)
XLA Ops:
  0.0 0.0 copy-start.7
  0.0 0.0 copy-start.6
  0.0 0.7 %copy-done.7 = f32[256]{0:T(256)S(1)} copy-done((f32[256]{0:T(256)S(1)}, f32[256]{0:T(256)}, u32[]{:S(2)}) %copy-start.7) | copy-done | bytes 1048
  0.7 0.0 copy-done.6
  0.7 0.0 copy-start
  0.7 1.0 %copy-done = bf16[1024,256]{1,0:T(8,128)(2,1)S(1)} copy-done((bf16[1024,256]{1,0:T(8,128)(2,1)S(1)}, bf16[1024,256]{1,0:T(8,128)(2,1)}, u32[]{:S(2)}) %copy-start) | copy-done | bytes 524312
  1.7 0.0 copy-start.1
  1.7 0.9 %copy-done.1 = bf16[512,256]{1,0:T(8,128)(2,1)S(1)} copy-done((bf16[512,256]{1,0:T(8,128)(2,1)S(1)}, bf16[512,256]{1,0:T(8,128)(2,1)}, u32[]{:S(2)}) %copy-start.1) | copy-done | bytes 262168
  2.7 0.0 copy-start.2
  2.7 0.9 %copy-done.2 = bf16[512,256]{1,0:T(8,128)(2,1)S(1)} copy-done((bf16[512,256]{1,0:T(8,128)(2,1)S(1)}, bf16[512,256]{1,0:T(8,128)(2,1)}, u32[]{:S(2)}) %copy-start.2) | copy-done | bytes 262168
  3.6 0.0 copy-start.3
  3.6 0.9 %copy-done.3 = bf16[512,256]{1,0:T(8,128)(2,1)S(1)} copy-done((bf16[512,256]{1,0:T(8,128)(2,1)S(1)}, bf16[512,256]{1,0:T(8,128)(2,1)}, u32[]{:S(2)}) %copy-start.3) | copy-done | bytes 262168
  4.6 0.0 copy-start.4
  4.6 0.7 %copy-done.4 = f32[16,256]{1,0:T(8,128)S(1)} copy-done((f32[16,256]{1,0:T(8,128)S(1)}, f32[16,256]{1,0:T(8,128)}, u32[]{:S(2)}) %copy-start.4) | copy-done | bytes 16408
  5.3 0.0 copy-start.5
  5.3 0.7 %copy-done.5 = f32[16,256]{1,0:T(8,128)S(1)} copy-done((f32[16,256]{1,0:T(8,128)S(1)}, f32[16,256]{1,0:T(8,128)}, u32[]{:S(2)}) %copy-start.5) | copy-done | bytes 16408
  6.0 32.0 %layer.1 = bf16[512,256]{1,0:T(8,128)(2,1)S(1)} custom-call(bf16[512,256]{1,0:T(8,128)(2,1)S(1)} %copy-done.1, bf16[512,256]{1,0:T(8,128)(2,1)S(1)} %copy-done.2, bf16[512,256]{1,0:T(8,128)(2,1)S(1)} %copy-done.3, f32[16,256]{1,0:T(8,128)S(1)} %copy-done.4, f32[16,256]{1,0:T(8,128)S(1)} %copy-done.5, f32[1,256]{1,0:T(1,128)S(1)} %bitcast.2, ...), custom_call_target="tpu_custom_call" | custom-call | tf_op jit(solution)/shard_map/layer/pallas_call | solution.py:268
  38.1 0.7 %copy.10 = bf16[512,256]{1,0:T(8,128)(2,1)} copy(bf16[512,256]{1,0:T(8,128)(2,1)S(1)} %layer.1) | data formatting | bytes 524288
Async XLA Ops:
  0.0 0.7 %copy-start.7 = (f32[256]{0:T(256)S(1)}, f32[256]{0:T(256)}, u32[]{:S(2)}) copy-start(f32[256]{0:T(256)} %param.15) | copy-start | bytes 3076
  0.0 0.7 %copy-start.6 = (f32[256]{0:T(256)S(1)}, f32[256]{0:T(256)}, u32[]{:S(2)}) copy-start(f32[256]{0:T(256)} %param.13) | copy-start | bytes 3076
  0.7 1.0 %copy-start = (bf16[1024,256]{1,0:T(8,128)(2,1)S(1)}, bf16[1024,256]{1,0:T(8,128)(2,1)}, u32[]{:S(2)}) copy-start(bf16[1024,256]{1,0:T(8,128)(2,1)} %w_hbm.1) | copy-start | bytes 1572868
  1.7 0.9 %copy-start.1 = (bf16[512,256]{1,0:T(8,128)(2,1)S(1)}, bf16[512,256]{1,0:T(8,128)(2,1)}, u32[]{:S(2)}) copy-start(bf16[512,256]{1,0:T(8,128)(2,1)} %q_hbm.1) | copy-start | bytes 786436
  2.7 0.9 %copy-start.2 = (bf16[512,256]{1,0:T(8,128)(2,1)S(1)}, bf16[512,256]{1,0:T(8,128)(2,1)}, u32[]{:S(2)}) copy-start(bf16[512,256]{1,0:T(8,128)(2,1)} %k_hbm.1) | copy-start | bytes 786436
  3.6 0.9 %copy-start.3 = (bf16[512,256]{1,0:T(8,128)(2,1)S(1)}, bf16[512,256]{1,0:T(8,128)(2,1)}, u32[]{:S(2)}) copy-start(bf16[512,256]{1,0:T(8,128)(2,1)} %v_hbm.1) | copy-start | bytes 786436
  4.6 0.7 %copy-start.4 = (f32[16,256]{1,0:T(8,128)S(1)}, f32[16,256]{1,0:T(8,128)}, u32[]{:S(2)}) copy-start(f32[16,256]{1,0:T(8,128)} %decay_ref.1) | copy-start | bytes 49156
  5.3 0.7 %copy-start.5 = (f32[16,256]{1,0:T(8,128)S(1)}, f32[16,256]{1,0:T(8,128)}, u32[]{:S(2)}) copy-start(f32[16,256]{1,0:T(8,128)} %residue_ref.1) | copy-start | bytes 49156
where the time goes:
time: 39.3 us; the launch traced here: 38.8 us
  Pallas kernels  32 us (81%)
  local copies, waits for them, and re-layouts  6.72 us (17%)
    pallas_call x1, Pallas kernels, layer(): pl.pallas_call(kernel, out_shape=jax.ShapeDtypeStruct((tokens, channels),...  32 us
    unnamed x17, local copies, waits for them, and re-layouts  6.72 us

commit v1 on v0

v1 whole, which is shorter than its diff:
```python
import functools

import jax
import jax.numpy as jnp
from jax import lax
from jax.experimental import pallas as pl
from jax.experimental.pallas import tpu as pltpu
from jax.sharding import PartitionSpec as P

MESH = pl.DeviceIdType.MESH
F32 = jnp.float32
BF16 = jnp.bfloat16
NX, NZ, NC, NY = 4, 8, 2, 4
SUB = 8
LANES = 128
CHUNKS = 8
EARLY = 4


def tree(terms):
    while len(terms) > 1:
        terms = [a + b for a, b in zip(terms[::2], terms[1::2])] + terms[len(terms) // 2 * 2 :]
    return terms[0]


def rows_of(array, n, lane):
    return jnp.broadcast_to(array[n : n + 1, lane : lane + LANES], (SUB, LANES))


def kernel(
    q_hbm, k_hbm, v_hbm, decay_hbm, residue_hbm, skip_hbm, w_hbm, bias_hbm, out_ref,
    decay_ref, residue_ref, skip_ref, bias_ref, k_buf, v_buf, q_buf, w_buf, u_buf, qf_buf, y_buf, h_buf, lam_buf, sub_buf,
    q_peer, y_peer, d_peer, c_peer, g_peer,
    z_buf, x_buf, mate_s, mate_pre, t_buf, p_buf, gathered, o_buf,
    load_sem, z_ready, x_ready, z_send, z_recv, x_send, x_recv, mate_send, mate_recv, y_send, y_recv,
    d_send, d_recv, q_send, q_recv, l_send, l_recv, c_send, c_recv,
):
    modes, channels = decay_ref.shape
    tokens = u_buf.shape[1]
    steps = tokens // SUB
    part = steps // CHUNKS
    early = EARLY * part
    lane_starts = range(0, channels, LANES)
    seq = lax.axis_index("seq")
    y = lax.axis_index("chan")
    x, z, core = seq // (NZ * NC), (seq // NC) % NZ, seq % NC

    def device(xx, zz, cc, yy):
        return ((xx * NZ + zz) * NC + cc, yy)

    loads = [
        pltpu.make_async_copy(src, dst, load_sem.at[i])
        for i, (src, dst) in enumerate(
            [
                (k_hbm, k_buf), (v_hbm, v_buf), (decay_hbm, decay_ref), (residue_hbm, residue_ref),
                (skip_hbm, skip_ref), (q_hbm, q_buf), (w_hbm, w_buf), (bias_hbm, bias_ref),
            ]
        )
    ]
    for load in loads:
        load.start()

    x_buf[...] = jnp.zeros_like(x_buf)
    z_buf[...] = jnp.zeros_like(z_buf)
    mate = device(x, z, 1 - core, y)
    y_peers = [device(x, z, core, (y + k) % NY) for k in (2, 1, 3)]
    barrier = pltpu.get_barrier_semaphore()

    def tell(semaphore, where):
        pl.semaphore_signal(semaphore, inc=1, device_id=where, device_id_type=MESH)

    for where in y_peers + [mate]:
        tell(barrier, where)
    for k in range(1, NZ):
        @pl.when(z + k < NZ)
        def _(k=k):
            tell(barrier, device(x, z + k, core, y))
    for k in range(1, NX):
        @pl.when(x + k < NX)
        def _(k=k):
            for cc in range(NC):
                tell(barrier, device(x + k, z, cc, y))
    pl.semaphore_wait(barrier, NY + z + NC * x)
    for k in range(1, NZ):
        @pl.when(z >= k)
        def _(k=k):
            tell(z_ready.at[z], device(x, z - k, core, y))
    for k in range(1, NX):
        @pl.when(x >= k)
        def _(k=k):
            for cc in range(NC):
                tell(x_ready.at[x, core], device(x - k, z, cc, y))

    def along_y(src, dst, send, recv):
        copies = [
            pltpu.make_async_remote_copy(
                src_ref=src, dst_ref=dst, send_sem=send.at[i], recv_sem=recv.at[y],
                device_id=where, device_id_type=MESH,
            )
            for i, where in enumerate(y_peers)
        ]
        for copy in copies:
            copy.start()
        y_copies.extend(copies)

    def from_y(src, dst, recv):
        pltpu.make_async_remote_copy(
            src_ref=dst, dst_ref=dst, send_sem=q_send.at[0], recv_sem=recv.at[src],
            device_id=mate, device_id_type=MESH,
        ).wait_recv()

    y_copies = []
    others = [(y + k) % NY for k in (1, 3, 2)]
    along_y(q_hbm.at[:, pl.ds(0, early)], q_peer.at[y], q_send, q_recv)

    loads[2].wait()
    decay = decay_ref[...]
    d_peer[y] = decay
    along_y(d_peer.at[y], d_peer.at[y], d_send, d_recv)
    lam_buf[y] = jnp.exp(-decay)

    loads[0].wait()
    loads[1].wait()
    for lane in lane_starts:
        k_part, v_part = (buf[:, pl.ds(lane, LANES)].astype(F32) for buf in (k_buf, v_buf))
        u_buf[lane // LANES] = (k_part * v_part).astype(BF16).astype(F32)

    sublane = lax.broadcasted_iota(jnp.int32, (SUB, LANES), 0)
    for lane in lane_starts:
        lam = [rows_of(lam_buf[y], n, lane) for n in range(modes)]

        def advance(b, state, lam=lam, lane=lane):
            u = u_buf[lane // LANES, pl.ds(b, SUB, stride=steps), :]
            return tuple(l * h + u for l, h in zip(lam, state))

        zero = jnp.zeros((SUB, LANES), F32)
        state = lax.fori_loop(0, steps, advance, (zero,) * modes, unroll=8)
        for n in range(modes):
            run = state[n]
            for shift in (1, 2, 4):
                factor = jnp.exp(-rows_of(decay, n, lane) * float(steps * shift))
                moved = jnp.where(sublane >= shift, pltpu.roll(run, shift, 0), 0.0)
                run = run + factor * moved
            z_buf[pl.ds(z, 1), pl.ds(n, 1), pl.ds(lane, LANES)] = run[SUB - 1 : SUB].reshape(1, 1, LANES)
            h_buf[n, :, pl.ds(lane, LANES)] = jnp.where(sublane >= 1, pltpu.roll(run, 1, 0), 0.0)

    def state_copy(slot, target):
        return pltpu.make_async_remote_copy(
            src_ref=z_buf.at[slot], dst_ref=z_buf.at[slot],
            send_sem=z_send.at[target], recv_sem=z_recv.at[slot],
            device_id=device(x, target, core, y), device_id_type=MESH,
        )

    def send_forward(k):
        pl.semaphore_wait(z_ready.at[z + k], 1)
        state_copy(z, z + k).start()

    needs_total = x < NX - 1
    half = NZ // 2
    s_copy = pltpu.make_async_remote_copy(
        src_ref=z_buf.at[z], dst_ref=mate_s, send_sem=mate_send.at[0], recv_sem=mate_recv.at[0],
        device_id=mate, device_id_type=MESH,
    )
    for k in (4, 3, 5, 2, 6, 1, 7):
        @pl.when((z >= k) & needs_total)
        def _(k=k):
            state_copy(z, z - k).start()
    for k in range(1, half):
        @pl.when((z + k < half) | ((z >= half) & (z + k < NZ)))
        def _(k=k):
            send_forward(k)
    s_copy.start()

    loads[3].wait()
    loads[4].wait()
    for lane in lane_starts:
        lam = [rows_of(lam_buf[y], n, lane) for n in range(modes)]
        weight = [rows_of(residue_ref[...], n, lane) for n in range(modes)]
        skip_row = jnp.broadcast_to(skip_ref[:, lane : lane + LANES], (SUB, LANES))

        def local(b, state, lam=lam, weight=weight, skip_row=skip_row, lane=lane):
            u = u_buf[lane // LANES, pl.ds(b, SUB, stride=steps), :]
            state = tuple(l * h + u for l, h in zip(lam, state))
            y_buf[b, :, pl.ds(lane, LANES)] = tree([w * h for w, h in zip(weight, state)] + [skip_row * u])
            return state

        first = tuple(h_buf[n, :, pl.ds(lane, LANES)] for n in range(modes))
        last = lax.fori_loop(0, early, local, first, unroll=4)
        y_peer[y, :, pl.ds(lane, LANES)] = (
            y_buf[pl.ds(0, early), :, pl.ds(lane, LANES)].reshape(early * SUB, LANES).astype(BF16)
        )
        for n in range(modes):
            h_buf[n, :, pl.ds(lane, LANES)] = last[n]
    along_y(y_peer.at[y], y_peer.at[y], l_send, l_recv)
    for lane in lane_starts:
        lam = [rows_of(lam_buf[y], n, lane) for n in range(modes)]
        weight = [rows_of(residue_ref[...], n, lane) for n in range(modes)]
        skip_row = jnp.broadcast_to(skip_ref[:, lane : lane + LANES], (SUB, LANES))

        def local(b, state, lam=lam, weight=weight, skip_row=skip_row, lane=lane):
            u = u_buf[lane // LANES, pl.ds(b, SUB, stride=steps), :]
            state = tuple(l * h + u for l, h in zip(lam, state))
            y_buf[b, :, pl.ds(lane, LANES)] = tree([w * h for w, h in zip(weight, state)] + [skip_row * u])
            return state

        first = tuple(h_buf[n, :, pl.ds(lane, LANES)] for n in range(modes))
        lax.fori_loop(early, steps, local, first, unroll=4)
        for n in range(modes):
            place = (sublane * steps + 1).astype(F32)
            sub_buf[y, n, :, pl.ds(lane, LANES)] = jnp.exp(-rows_of(decay, n, lane) * place)
    for k in range(1, NZ):
        @pl.when((z < half) & (z + k >= half) & (z + k < NZ))
        def _(k=k):
            send_forward(k)
    loads[5].wait()
    for lane in lane_starts:
        qf_buf[y, lane // LANES] = q_buf[:, :, pl.ds(lane, LANES)].astype(F32).reshape(tokens, LANES)

    chip_power = jnp.exp(-decay * float(NC * tokens))
    row_power = jnp.exp(-decay * float(NZ * NC * tokens))
    half_power = jnp.exp(-decay * float(tokens))
    place_power = jnp.exp(-decay * (z * (NC * tokens)).astype(F32))

    for k in range(1, NZ):
        @pl.when(z >= k)
        def _(k=k):
            state_copy(z - k, z).wait_recv()

        @pl.when((z + k < NZ) & needs_total)
        def _(k=k):
            state_copy(z + k, z).wait_recv()
    total = jnp.zeros_like(decay)
    prefix = jnp.zeros_like(decay)
    for zz in range(NZ):
        prefix = jnp.where(z == zz, total, prefix)
        total = chip_power * total + z_buf[zz]
    t_buf[...] = total
    p_buf[...] = prefix

    def total_copy(slot, target, cc):
        return pltpu.make_async_remote_copy(
            src_ref=t_buf, dst_ref=x_buf.at[core, slot],
            send_sem=x_send.at[target, cc], recv_sem=x_recv.at[core, slot],
            device_id=device(target, z, cc, y), device_id_type=MESH,
        )

    for k in range(1, NX):
        @pl.when(x + k < NX)
        def _(k=k):
            for cc in range(NC):
                pl.semaphore_wait(x_ready.at[x + k, cc], 1)
                total_copy(x, x + k, cc).start()
    p_copy = pltpu.make_async_remote_copy(
        src_ref=p_buf, dst_ref=mate_pre, send_sem=mate_send.at[1], recv_sem=mate_recv.at[1],
        device_id=mate, device_id_type=MESH,
    )
    p_copy.start()
    for src in others:
        from_y(src, q_peer.at[src], q_recv)
        from_y(src, d_peer.at[src], d_recv)
        lam_buf[src] = jnp.exp(-d_peer[src])
        for lane in lane_starts:
            for n in range(modes):
                place = (sublane * steps + 1).astype(F32)
                sub_buf[src, n, :, pl.ds(lane, LANES)] = jnp.exp(-rows_of(d_peer[src], n, lane) * place)
            for a in range(SUB):
                qf_buf[src, lane // LANES, pl.ds(a * steps, early), :] = q_peer[
                    src, a, :, pl.ds(lane, LANES)
                ].astype(F32)
    s_copy.wait()
    p_copy.wait()
    for k in range(1, NX):
        @pl.when(x >= k)
        def _(k=k):
            for cc in range(NC):
                pltpu.make_async_remote_copy(
                    src_ref=t_buf, dst_ref=x_buf.at[cc, x - k],
                    send_sem=x_send.at[0, 0], recv_sem=x_recv.at[cc, x - k],
                    device_id=mate, device_id_type=MESH,
                ).wait_recv()

    before = jnp.zeros_like(decay)
    for xx in range(NX - 1):
        step = half_power * x_buf[0, xx] + x_buf[1, xx]
        before = jnp.where(xx < x, row_power * before + step, before)
    other = mate_pre[...]
    first_core = jnp.where(core == 0, prefix, other)
    second_core = jnp.where(core == 0, other, prefix)
    carry = place_power * before + half_power * first_core + second_core
    carry = jnp.where(core == 0, carry, half_power * carry + mate_s[...])
    c_peer[y] = residue_ref[...] * carry
    along_y(c_peer.at[y], c_peer.at[y], c_send, c_recv)

    def start_carry(src):
        for lane in lane_starts:
            for n in range(modes):
                g_peer[n, :, pl.ds(lane, LANES)] = sub_buf[src, n, :, pl.ds(lane, LANES)] * rows_of(
                    c_peer[src], n, lane
                )

    def skip_early():
        for lane in lane_starts:
            for n in range(modes):
                ahead = jnp.exp(-rows_of(decay, n, lane) * float(early))
                g_peer[n, :, pl.ds(lane, LANES)] = g_peer[n, :, pl.ds(lane, LANES)] * ahead

    def finish(src, begin, end, local_at):
        for lane in lane_starts:
            lam = [rows_of(lam_buf[src], n, lane) for n in range(modes)]

            def step(i, state, lam=lam, lane=lane):
                b = begin + 2 * i
                local = local_at(b, lane)
                pair = []
                for o in range(2):
                    gate = qf_buf[src, lane // LANES, pl.ds(b + o, SUB, stride=steps), :]
                    pair.append(gate * tree(list(state) + [local[o]]))
                    state = tuple(l * h for l, h in zip(lam, state))
                rows = jnp.concatenate(pair, axis=0).astype(BF16)
                start = pl.multiple_of(b * SUB, 2 * SUB)
                gathered[src, pl.ds(start, 2 * SUB), pl.ds(lane, LANES)] = rows
                return state

            first = tuple(g_peer[n, :, pl.ds(lane, LANES)] for n in range(modes))
            last = lax.fori_loop(0, (end - begin) // 2, step, first, unroll=4)
            for n in range(modes):
                g_peer[n, :, pl.ds(lane, LANES)] = last[n]

    def own_local(b, lane):
        return [y_buf[b + o, :, pl.ds(lane, LANES)] for o in range(2)]

    def chunk_rows(j):
        return pl.ds(j * part * SUB, part * SUB)

    start_carry(y)
    skip_early()
    for j in range(EARLY, CHUNKS):
        finish(y, j * part, (j + 1) * part, own_local)
        for i, where in enumerate(y_peers):
            copy = pltpu.make_async_remote_copy(
                src_ref=gathered.at[y, chunk_rows(j)], dst_ref=gathered.at[y, chunk_rows(j)],
                send_sem=y_send.at[i, j], recv_sem=y_recv.at[y, j],
                device_id=where, device_id_type=MESH,
            )
            copy.start()
            y_copies.append(copy)
    start_carry(y)
    finish(y, 0, early, own_local)
    for src in others:
        from_y(src, y_peer.at[src], l_recv)
        from_y(src, c_peer.at[src], c_recv)
        start_carry(src)

        def sent_local(b, lane, src=src):
            start = pl.multiple_of(b * SUB, 2 * SUB)
            both = y_peer[src, pl.ds(start, 2 * SUB), pl.ds(lane, LANES)].astype(F32)
            return [both[:SUB], both[SUB:]]

        finish(src, 0, early, sent_local)

    loads[6].wait()
    loads[7].wait()
    bias = jnp.broadcast_to(bias_ref[...], (part * SUB, channels))
    for j in range(CHUNKS):
        if j >= EARLY:
            for src in others:
                pltpu.make_async_remote_copy(
                    src_ref=gathered.at[src, chunk_rows(j)], dst_ref=gathered.at[src, chunk_rows(j)],
                    send_sem=q_send.at[0], recv_sem=y_recv.at[src, j],
                    device_id=mate, device_id_type=MESH,
                ).wait_recv()
        projected = bias
        for yy in range(NY):
            projected = projected + jnp.dot(
                gathered[yy, chunk_rows(j), :], w_buf[pl.ds(yy * channels, channels), :], preferred_element_type=F32
            )
        for i in range(part):
            for lane in lane_starts:
                o_buf[lane // LANES, pl.ds(j * part + i, SUB, stride=steps), :] = projected[
                    i * SUB : (i + 1) * SUB, lane : lane + LANES
                ]
    for lane in lane_starts:
        out_ref[:, pl.ds(lane, LANES)] = o_buf[lane // LANES].astype(BF16)

    for copy in y_copies:
        copy.wait_send()
    for k in range(1, NZ):
        @pl.when(z + k < NZ)
        def _(k=k):
            state_copy(z, z + k).wait_send()

        @pl.when((z >= k) & needs_total)
        def _(k=k):
            state_copy(z, z - k).wait_send()
    for k in range(1, NX):
        @pl.when(x + k < NX)
        def _(k=k):
            for cc in range(NC):
                total_copy(x, x + k, cc).wait_send()


def layer(q_gate, k_gate, value, decay, residue, skip, out_weight, out_bias):
    tokens, channels = q_gate.shape
    modes = decay.shape[0]
    steps = tokens // SUB
    early = EARLY * (steps // CHUNKS)
    dma = pltpu.SemaphoreType.DMA
    state = (modes, channels)
    any_spec = pl.BlockSpec(memory_space=pl.ANY)
    vmem = pl.BlockSpec(memory_space=pltpu.VMEM)
    return pl.pallas_call(
        kernel,
        out_shape=jax.ShapeDtypeStruct((tokens, channels), BF16),
        in_specs=[any_spec] * 8,
        out_specs=vmem,
        scratch_shapes=[
            pltpu.VMEM(state, F32),
            pltpu.VMEM(state, F32),
            pltpu.VMEM((1, channels), F32),
            pltpu.VMEM((1, channels), F32),
            pltpu.VMEM((tokens, channels), BF16),
            pltpu.VMEM((tokens, channels), BF16),
            pltpu.VMEM((SUB, steps, channels), BF16),
            pltpu.VMEM(out_weight.shape, BF16),
            pltpu.VMEM((channels // LANES, tokens, LANES), F32),
            pltpu.VMEM((NY, channels // LANES, tokens, LANES), F32),
            pltpu.VMEM((steps, SUB, channels), F32),
            pltpu.VMEM((modes, SUB, channels), F32),
            pltpu.VMEM((NY,) + state, F32),
            pltpu.VMEM((NY, modes, SUB, channels), F32),
            pltpu.VMEM((NY, SUB, early, channels), BF16),
            pltpu.VMEM((NY, early * SUB, channels), BF16),
            pltpu.VMEM((NY,) + state, F32),
            pltpu.VMEM((NY,) + state, F32),
            pltpu.VMEM((modes, SUB, channels), F32),
            pltpu.VMEM((NZ,) + state, F32),
            pltpu.VMEM((NC, NX) + state, F32),
            pltpu.VMEM(state, F32),
            pltpu.VMEM(state, F32),
            pltpu.VMEM(state, F32),
            pltpu.VMEM(state, F32),
            pltpu.VMEM((NY, tokens, channels), BF16),
            pltpu.VMEM((channels // LANES, tokens, LANES), F32),
            dma((8,)), pltpu.SemaphoreType.REGULAR((NZ,)), pltpu.SemaphoreType.REGULAR((NX, NC)),
            dma((NZ,)), dma((NZ,)), dma((NX, NC)), dma((NC, NX)),
            dma((2,)), dma((2,)), dma((NY - 1, CHUNKS)), dma((NY, CHUNKS)),
        ]
        + [dma((count,)) for _ in range(4) for count in (NY - 1, NY)],
        compiler_params=pltpu.CompilerParams(
            collective_id=0, has_side_effects=True, vmem_limit_bytes=62 * 2**20
        ),
        name="layer",
    )(q_gate.reshape(SUB, steps, channels), k_gate, value, decay, residue, skip.reshape(1, -1), out_weight, out_bias.reshape(1, -1))


def solution(mesh):
    return jax.shard_map(
        layer,
        mesh=mesh,
        in_specs=(
            P("seq", "chan"),
            P("seq", "chan"),
            P("seq", "chan"),
            P(None, "chan"),
            P(None, "chan"),
            P("chan"),
            P(None, "chan"),
            P("chan"),
        ),
        out_specs=P("seq", "chan"),
        check_vma=False,
    )
```

time: 39.3 us -> 29.8 us (0.76); the launches traced: 38.8 us -> 29.7 us
  local copies, waits for them, and re-layouts: 6.72 us -> 1.67 us
  Pallas kernels: 32 us -> 28 us
    unnamed x17 -> x1, local copies, waits for them, and re-layouts: 6.72 us -> 1.67 us
    pallas_call x1, Pallas kernels: 32 us -> 28 us  [layer(): pl.pallas_call(kernel, out_shape=jax.ShapeDtypeStruct((tokens, channels),...]
where the time goes in v1:
time: 29.8 us; the launch traced here: 29.7 us
  Pallas kernels  28 us (94%)
  local copies, waits for them, and re-layouts  1.67 us (6%)
    pallas_call x1, Pallas kernels, layer(): pl.pallas_call(kernel, out_shape=jax.ShapeDtypeStruct((tokens, channels),...  28 us
    unnamed x1, local copies, waits for them, and re-layouts  1.67 us

profile of v1, /device:TPU:6, one launch (start us, length us, event | category | flops | bytes accessed | tf_op | source)
XLA Modules:
  0.0 29.7 jit_solution(10880488515631669418)
XLA Ops:
  0.0 28.0 %layer.1 = bf16[512,256]{1,0:T(8,128)(2,1)} custom-call(bf16[8,64,256]{2,1,0:T(8,128)(2,1)} %bitcast.3, bf16[512,256]{1,0:T(8,128)(2,1)} %k_hbm.1, bf16[512,256]{1,0:T(8,128)(2,1)} %v_hbm.1, f32[16,256]{1,0:T(8,128)} %decay_hbm.1, f32[16,256]{1,0:T(8,128)} %residue_hbm.1, f32[1,256]{1,0:T(1,128)} %bitcast.4, bf16[1024,256]{1,0:T(8,128)(2,1)} %w_hbm.1, ...), custom_call_target="tpu_custom_call" | custom-call | tf_op jit(solution)/shard_map/layer/pallas_call | solution.py:411
  28.0 1.7 %copy.10 = bf16[512,256]{1,0:T(8,128)(2,1)} copy(bf16[512,256]{1,0:T(8,128)(2,1)} %layer.1) | data formatting | bytes 524288

commit v2 on v1

v2 whole, which is shorter than its diff:
```python
import functools

import jax
import jax.numpy as jnp
from jax import lax
from jax.experimental import pallas as pl
from jax.experimental.pallas import tpu as pltpu
from jax.sharding import PartitionSpec as P

MESH = pl.DeviceIdType.MESH
F32 = jnp.float32
BF16 = jnp.bfloat16
NX, NZ, NC, NY = 4, 8, 2, 4
SUB = 8
LANES = 128
CHUNKS = 8
LAG_EARLY, LEAD_EARLY = 4, 5


def tree(terms):
    while len(terms) > 1:
        terms = [a + b for a, b in zip(terms[::2], terms[1::2])] + terms[len(terms) // 2 * 2 :]
    return terms[0]


def rows_of(array, n, lane):
    return jnp.broadcast_to(array[n : n + 1, lane : lane + LANES], (SUB, LANES))


def kernel(
    q_hbm, k_hbm, v_hbm, decay_hbm, residue_hbm, skip_hbm, w_hbm, bias_hbm, out_ref,
    decay_ref, residue_ref, skip_ref, bias_ref, k_buf, v_buf, q_buf, w_buf,
    u_buf, qf_buf, y_buf, h_buf, lam_buf, sub_buf, g_buf,
    q_all, l_all, d_all, c_all, gathered, z_buf, x_buf, mate_s, mate_pre, t_buf, p_buf, o_buf,
    load_sem, mate_ready, y_ready, z_ready, x_ready, z_send, z_recv, x_send, x_recv, mate_send, mate_recv,
    late_send, late_recv, small_send, small_recv, ring_send, ring_recv,
):
    modes, channels = decay_ref.shape
    tokens = u_buf.shape[1]
    steps = tokens // SUB
    part = steps // CHUNKS
    lane_starts = range(0, channels, LANES)
    seq = lax.axis_index("seq")
    y = lax.axis_index("chan")
    x, z, core = seq // (NZ * NC), (seq // NC) % NZ, seq % NC
    half = NZ // 2
    lead = z < half
    following, previous, opposite = [(y + k) % NY for k in (1, 3, 2)]
    others = (following, previous, opposite)

    def device(xx, zz, cc, yy):
        return ((xx * NZ + zz) * NC + cc, yy)

    mate = device(x, z, 1 - core, y)

    def remote(src, dst, send, recv, where):
        return pltpu.make_async_remote_copy(
            src_ref=src, dst_ref=dst, send_sem=send, recv_sem=recv, device_id=where, device_id_type=MESH
        )

    def tell(semaphore, where):
        pl.semaphore_signal(semaphore, inc=1, device_id=where, device_id_type=MESH)

    loads = [
        pltpu.make_async_copy(src, dst, load_sem.at[i])
        for i, (src, dst) in enumerate(
            [
                (k_hbm, k_buf), (v_hbm, v_buf), (decay_hbm, decay_ref), (residue_hbm, residue_ref),
                (skip_hbm, skip_ref), (q_hbm, q_buf), (w_hbm, w_buf), (bias_hbm, bias_ref),
            ]
        )
    ]
    for load in loads:
        load.start()

    x_buf[...] = jnp.zeros_like(x_buf)
    z_buf[...] = jnp.zeros_like(z_buf)

    barrier = pltpu.get_barrier_semaphore()
    for k in range(1, NY):
        @pl.when(y + k < NY)
        def _(k=k):
            tell(barrier, device(x, z, core, y + k))

    @pl.when(core == 1)
    def _():
        tell(barrier, mate)

    for k in range(1, NZ):
        @pl.when(z + k < NZ)
        def _(k=k):
            tell(barrier, device(x, z + k, core, y))
    for k in range(1, NX):
        @pl.when(x + k < NX)
        def _(k=k):
            for cc in range(NC):
                tell(barrier, device(x + k, z, cc, y))
    earlier = 1 - core + y + z + NC * x

    @pl.when(earlier > 0)
    def _():
        pl.semaphore_wait(barrier, earlier)

    for k in range(1, NZ):
        @pl.when(z >= k)
        def _(k=k):
            tell(z_ready.at[z], device(x, z - k, core, y))
    for k in range(1, NX):
        @pl.when(x >= k)
        def _(k=k):
            for cc in range(NC):
                tell(x_ready.at[x, core], device(x - k, z, cc, y))
    for k in range(1, NY):
        @pl.when(y >= k)
        def _(k=k):
            tell(y_ready.at[y], device(x, z, core, y - k))

    @pl.when(core == 0)
    def _():
        tell(mate_ready, mate)

    spans = [(0, LAG_EARLY * part), (LAG_EARLY * part, LEAD_EARLY * part)]

    def rows(begin, end):
        return pl.ds(begin * SUB, (end - begin) * SUB)

    def hop(t, p, slot, which, target, i):
        begin, end = spans[p]
        size = (end - begin) * SUB // 2
        piece = (q_all, l_all)[t].at[slot, pl.ds(begin * SUB + which * size, size)]
        return remote(piece, piece, ring_send.at[t, p, i], ring_recv.at[t, p, slot, which], device(x, z, core, target))

    def own_hops(t, p):
        order = [(0, following), (1, previous), (1, following), (0, previous)]
        return [hop(t, p, y, which, target, i) for i, (which, target) in enumerate(order)]

    def forward_hops(t, p):
        return [hop(t, p, previous, 0, following, 4), hop(t, p, following, 1, previous, 5)]

    def ring_start(t, p):
        for copy in own_hops(t, p):
            copy.start()

    def ring_forward(t, p):
        for copy in forward_hops(t, p):
            copy.wait_recv()
            copy.start()

    def ring_finish(t, p):
        for slot, which in [(previous, 1), (following, 0), (opposite, 0), (opposite, 1)]:
            hop(t, p, slot, which, following, 0).wait_recv()

    def small_hops(t, buf, slot):
        return [
            remote(buf.at[slot], buf.at[slot], small_send.at[t, i], small_recv.at[t, slot], device(x, z, core, (y + k) % NY))
            for i, k in enumerate((2, 1, 3))
        ]

    def small_wait(t, buf, slot):
        remote(buf.at[slot], buf.at[slot], small_send.at[t, 0], small_recv.at[t, slot], mate).wait_recv()

    def late_hops(j):
        piece = gathered.at[y, rows(j * part, (j + 1) * part)]
        return [
            remote(piece, piece, late_send.at[i, j], late_recv.at[y, j], device(x, z, core, (y + k) % NY))
            for i, k in enumerate((2, 1, 3))
        ]

    def send_gate():
        loads[5].wait()
        for lane in lane_starts:
            qf_buf[lane // LANES] = q_buf[:, pl.ds(lane, LANES)].astype(F32)
        for lane in lane_starts:

            def spread(i, carry, lane=lane):
                pair = [qf_buf[lane // LANES, pl.ds(2 * i + o, SUB, stride=steps), :] for o in range(2)]
                start = pl.multiple_of(i * 2 * SUB, 2 * SUB)
                q_all[y, pl.ds(start, 2 * SUB), pl.ds(lane, LANES)] = jnp.concatenate(pair, axis=0).astype(BF16)
                return carry

            lax.fori_loop(0, steps // 2, spread, 0, unroll=8)
        ring_start(0, 0)

        @pl.when(lead)
        def _():
            ring_start(0, 1)

    loads[2].wait()
    decay = decay_ref[...]
    lam_buf[y] = jnp.exp(-decay)

    loads[0].wait()
    loads[1].wait()
    for lane in lane_starts:
        k_part, v_part = (buf[:, pl.ds(lane, LANES)].astype(F32) for buf in (k_buf, v_buf))
        u_buf[lane // LANES] = (k_part * v_part).astype(BF16).astype(F32)

    sublane = lax.broadcasted_iota(jnp.int32, (SUB, LANES), 0)
    for lane in lane_starts:
        lam = [rows_of(lam_buf[y], n, lane) for n in range(modes)]

        def advance(b, state, lam=lam, lane=lane):
            u = u_buf[lane // LANES, pl.ds(b, SUB, stride=steps), :]
            return tuple(l * h + u for l, h in zip(lam, state))

        zero = jnp.zeros((SUB, LANES), F32)
        state = lax.fori_loop(0, steps, advance, (zero,) * modes, unroll=8)
        for n in range(modes):
            run = state[n]
            for shift in (1, 2, 4):
                factor = jnp.exp(-rows_of(decay, n, lane) * float(steps * shift))
                moved = jnp.where(sublane >= shift, pltpu.roll(run, shift, 0), 0.0)
                run = run + factor * moved
            z_buf[pl.ds(z, 1), pl.ds(n, 1), pl.ds(lane, LANES)] = run[SUB - 1 : SUB].reshape(1, 1, LANES)
            h_buf[n, :, pl.ds(lane, LANES)] = jnp.where(sublane >= 1, pltpu.roll(run, 1, 0), 0.0)

    def state_copy(slot, target):
        return remote(z_buf.at[slot], z_buf.at[slot], z_send.at[target], z_recv.at[slot], device(x, target, core, y))

    def send_forward(k):
        pl.semaphore_wait(z_ready.at[z + k], 1)
        state_copy(z, z + k).start()

    needs_total = x < NX - 1
    s_copy = remote(z_buf.at[z], mate_s, mate_send.at[0], mate_recv.at[0], mate)
    for k in (4, 3, 5, 2, 6, 1, 7):
        @pl.when((z >= k) & needs_total)
        def _(k=k):
            state_copy(z, z - k).start()
    for k in range(1, half):
        @pl.when(~lead & (z + k < NZ))
        def _(k=k):
            send_forward(k)

    @pl.when(core == 1)
    def _():
        pl.semaphore_wait(mate_ready, 1)

    s_copy.start()
    for k in range(1, NY):
        @pl.when(y + k < NY)
        def _(k=k):
            pl.semaphore_wait(y_ready.at[y + k], 1)
    send_gate()

    d_all[y] = decay
    for copy in small_hops(0, d_all, y):
        copy.start()

    loads[3].wait()
    loads[4].wait()
    for begin, end in [spans[0], (spans[0][1], steps)]:
        for lane in lane_starts:
            lam = [rows_of(lam_buf[y], n, lane) for n in range(modes)]
            weight = [rows_of(residue_ref[...], n, lane) for n in range(modes)]
            skip_row = jnp.broadcast_to(skip_ref[:, lane : lane + LANES], (SUB, LANES))

            def local(i, state, lam=lam, weight=weight, skip_row=skip_row, lane=lane):
                pair = []
                for o in range(2):
                    b = 2 * i + o
                    u = u_buf[lane // LANES, pl.ds(b, SUB, stride=steps), :]
                    state = tuple(l * h + u for l, h in zip(lam, state))
                    total = tree([w * h for w, h in zip(weight, state)] + [skip_row * u])
                    y_buf[b, :, pl.ds(lane, LANES)] = total
                    pair.append(total)
                start = pl.multiple_of(i * 2 * SUB, 2 * SUB)
                l_all[y, pl.ds(start, 2 * SUB), pl.ds(lane, LANES)] = jnp.concatenate(pair, axis=0).astype(BF16)
                return state

            first = tuple(h_buf[n, :, pl.ds(lane, LANES)] for n in range(modes))
            last = lax.fori_loop(begin // 2, end // 2, local, first, unroll=2)
            for n in range(modes):
                h_buf[n, :, pl.ds(lane, LANES)] = last[n]
        if begin == 0:
            ring_start(1, 0)

    @pl.when(lead)
    def _():
        ring_start(1, 1)

    for k in range(1, NZ):
        @pl.when(lead & (z + k < NZ))
        def _(k=k):
            send_forward(k)

    @pl.when(lead)
    def _():
        ring_forward(0, 0)
        ring_forward(0, 1)


    place = (sublane * steps + 1).astype(F32)
    for lane in lane_starts:
        for n in range(modes):
            sub_buf[y, n, :, pl.ds(lane, LANES)] = jnp.exp(-rows_of(decay, n, lane) * place)
    chip_power = jnp.exp(-decay * float(NC * tokens))
    row_power = jnp.exp(-decay * float(NZ * NC * tokens))
    half_power = jnp.exp(-decay * float(tokens))
    place_power = jnp.exp(-decay * (z * (NC * tokens)).astype(F32))

    for k in range(1, NZ):
        @pl.when(z >= k)
        def _(k=k):
            state_copy(z - k, z).wait_recv()

        @pl.when((z + k < NZ) & needs_total)
        def _(k=k):
            state_copy(z + k, z).wait_recv()
    total = jnp.zeros_like(decay)
    prefix = jnp.zeros_like(decay)
    for zz in range(NZ):
        prefix = jnp.where(z == zz, total, prefix)
        total = chip_power * total + z_buf[zz]
    t_buf[...] = total
    p_buf[...] = prefix

    def total_copy(slot, target, cc):
        return remote(t_buf, x_buf.at[core, slot], x_send.at[target, cc], x_recv.at[core, slot], device(target, z, cc, y))

    for k in range(1, NX):
        @pl.when(x + k < NX)
        def _(k=k):
            for cc in range(NC):
                pl.semaphore_wait(x_ready.at[x + k, cc], 1)
                total_copy(x, x + k, cc).start()
    p_copy = remote(p_buf, mate_pre, mate_send.at[1], mate_recv.at[1], mate)
    p_copy.start()

    @pl.when(~lead)
    def _():
        ring_forward(0, 0)

    ring_forward(1, 0)

    @pl.when(lead)
    def _():
        ring_forward(1, 1)

    for src in others:
        small_wait(0, d_all, src)
        lam_buf[src] = jnp.exp(-d_all[src])
        for lane in lane_starts:
            for n in range(modes):
                sub_buf[src, n, :, pl.ds(lane, LANES)] = jnp.exp(-rows_of(d_all[src], n, lane) * place)
    s_copy.wait()
    p_copy.wait()
    for k in range(1, NX):
        @pl.when(x >= k)
        def _(k=k):
            for cc in range(NC):
                remote(t_buf, x_buf.at[cc, x - k], x_send.at[0, 0], x_recv.at[cc, x - k], mate).wait_recv()

    before = jnp.zeros_like(decay)
    for xx in range(NX - 1):
        step = half_power * x_buf[0, xx] + x_buf[1, xx]
        before = jnp.where(xx < x, row_power * before + step, before)
    other = mate_pre[...]
    first_core = jnp.where(core == 0, prefix, other)
    second_core = jnp.where(core == 0, other, prefix)
    carry = place_power * before + half_power * first_core + second_core
    carry = jnp.where(core == 0, carry, half_power * carry + mate_s[...])
    c_all[y] = residue_ref[...] * carry
    for copy in small_hops(1, c_all, y):
        copy.start()

    def start_carry(src, ahead=None):
        for lane in lane_starts:
            for n in range(modes):
                first = sub_buf[src, n, :, pl.ds(lane, LANES)] * rows_of(c_all[src], n, lane)
                if ahead is not None:
                    first = first * rows_of(ahead, n, lane)
                g_buf[n, :, pl.ds(lane, LANES)] = first

    def finish(src, begin, end, own):
        for lane in lane_starts:
            lam = [rows_of(lam_buf[src], n, lane) for n in range(modes)]

            def step(i, state, lam=lam, lane=lane):
                here = pl.ds(pl.multiple_of(i * 2 * SUB, 2 * SUB), 2 * SUB)
                gate = q_all[src, here, pl.ds(lane, LANES)].astype(F32)
                if own:
                    local = [y_buf[2 * i + o, :, pl.ds(lane, LANES)] for o in range(2)]
                else:
                    both = l_all[src, here, pl.ds(lane, LANES)].astype(F32)
                    local = [both[:SUB], both[SUB:]]
                pair = []
                for o in range(2):
                    pair.append(tree(list(state) + [local[o]]))
                    state = tuple(l * h for l, h in zip(lam, state))
                gathered[src, here, pl.ds(lane, LANES)] = (gate * jnp.concatenate(pair, axis=0)).astype(BF16)
                return state

            first = tuple(g_buf[n, :, pl.ds(lane, LANES)] for n in range(modes))
            last = lax.fori_loop(begin // 2, end // 2, step, first, unroll=4)
            for n in range(modes):
                g_buf[n, :, pl.ds(lane, LANES)] = last[n]

    def project(begin, end):
        projected = jnp.broadcast_to(bias_ref[...], ((end - begin) * SUB, channels))
        for yy in range(NY):
            projected = projected + jnp.dot(
                gathered[yy, rows(begin, end), :], w_buf[pl.ds(yy * channels, channels), :], preferred_element_type=F32
            )
        for i in range(end - begin):
            for lane in lane_starts:
                o_buf[lane // LANES, pl.ds(begin + i, SUB, stride=steps), :] = projected[
                    i * SUB : (i + 1) * SUB, lane : lane + LANES
                ]

    def late(first_late):
        for j in range(first_late, CHUNKS):
            finish(y, j * part, (j + 1) * part, True)
            for copy in late_hops(j):
                copy.start()

    start_carry(y, jnp.exp(-decay * jnp.where(lead, spans[1][1], spans[0][1]).astype(F32)))

    @pl.when(lead)
    def _():
        late(LEAD_EARLY)

    @pl.when(~lead)
    def _():
        late(LAG_EARLY)

    start_carry(y)
    finish(y, *spans[0], True)

    @pl.when(lead)
    def _():
        finish(y, *spans[1], True)

    for t in range(2):
        ring_finish(t, 0)

    @pl.when(lead)
    def _():
        for t in range(2):
            ring_finish(t, 1)

    for src in others:
        small_wait(1, c_all, src)
        start_carry(src)
        finish(src, *spans[0], False)

        @pl.when(lead)
        def _(src=src):
            finish(src, *spans[1], False)

    loads[6].wait()
    loads[7].wait()
    project(*spans[0])

    @pl.when(lead)
    def _():
        project(*spans[1])

    def project_late(first_late):
        for j in range(first_late, CHUNKS, 2):
            end = min(j + 2, CHUNKS)
            for i in range(j, end):
                for src in others:
                    piece = gathered.at[src, rows(i * part, (i + 1) * part)]
                    remote(piece, piece, late_send.at[0, i], late_recv.at[src, i], mate).wait_recv()
            project(j * part, end * part)

    @pl.when(lead)
    def _():
        project_late(LEAD_EARLY)

    @pl.when(~lead)
    def _():
        project_late(LAG_EARLY)

    for lane in lane_starts:
        out_ref[:, pl.ds(lane, LANES)] = o_buf[lane // LANES].astype(BF16)

    def sent(copies):
        for copy in copies:
            copy.wait_send()

    sent(small_hops(0, d_all, y) + small_hops(1, c_all, y))
    for t in range(2):
        sent(own_hops(t, 0) + forward_hops(t, 0))
    for j in range(LEAD_EARLY, CHUNKS):
        sent(late_hops(j))

    @pl.when(lead)
    def _():
        for t in range(2):
            sent(own_hops(t, 1) + forward_hops(t, 1))

    @pl.when(~lead)
    def _():
        for j in range(LAG_EARLY, LEAD_EARLY):
            sent(late_hops(j))

    for k in range(1, NZ):
        @pl.when(z + k < NZ)
        def _(k=k):
            state_copy(z, z + k).wait_send()

        @pl.when((z >= k) & needs_total)
        def _(k=k):
            state_copy(z, z - k).wait_send()
    for k in range(1, NX):
        @pl.when(x + k < NX)
        def _(k=k):
            for cc in range(NC):
                total_copy(x, x + k, cc).wait_send()


def layer(q_gate, k_gate, value, decay, residue, skip, out_weight, out_bias):
    tokens, channels = q_gate.shape
    modes = decay.shape[0]
    steps = tokens // SUB
    dma = pltpu.SemaphoreType.DMA
    regular = pltpu.SemaphoreType.REGULAR
    state = (modes, channels)
    by_lane = (channels // LANES, tokens, LANES)
    by_sublane = (modes, SUB, channels)
    any_spec = pl.BlockSpec(memory_space=pl.ANY)
    shapes = [
        (state, F32), (state, F32), ((1, channels), F32), ((1, channels), F32),
        ((tokens, channels), BF16), ((tokens, channels), BF16), ((tokens, channels), BF16),
        (out_weight.shape, BF16), (by_lane, F32), (by_lane, F32),
        ((steps, SUB, channels), F32), (by_sublane, F32),
        ((NY,) + state, F32), ((NY,) + by_sublane, F32), (by_sublane, F32),
        ((NY, tokens, channels), BF16), ((NY, tokens, channels), BF16),
        ((NY,) + state, F32), ((NY,) + state, F32),
        ((NY, tokens, channels), BF16),
        ((NZ,) + state, F32), ((NC, NX) + state, F32),
        (state, F32), (state, F32), (state, F32), (state, F32),
        (by_lane, F32),
    ]
    return pl.pallas_call(
        kernel,
        out_shape=jax.ShapeDtypeStruct((tokens, channels), BF16),
        in_specs=[any_spec] * 8,
        out_specs=pl.BlockSpec(memory_space=pltpu.VMEM),
        scratch_shapes=[pltpu.VMEM(*shape) for shape in shapes]
        + [
            dma((8,)), regular, regular((NY,)), regular((NZ,)), regular((NX, NC)), dma((NZ,)), dma((NZ,)), dma((NX, NC)), dma((NC, NX)),
            dma((2,)), dma((2,)), dma((NY - 1, CHUNKS)), dma((NY, CHUNKS)),
            dma((2, NY - 1)), dma((2, NY)), dma((2, 2, 6)), dma((2, 2, NY, 2)),
        ],
        compiler_params=pltpu.CompilerParams(
            collective_id=0, has_side_effects=True, vmem_limit_bytes=62 * 2**20
        ),
        name="layer",
    )(q_gate, k_gate, value, decay, residue, skip.reshape(1, -1), out_weight, out_bias.reshape(1, -1))


def solution(mesh):
    return jax.shard_map(
        layer,
        mesh=mesh,
        in_specs=(
            P("seq", "chan"),
            P("seq", "chan"),
            P("seq", "chan"),
            P(None, "chan"),
            P(None, "chan"),
            P("chan"),
            P(None, "chan"),
            P("chan"),
        ),
        out_specs=P("seq", "chan"),
        check_vma=False,
    )
```

time: 29.8 us -> 28.8 us (0.966)
  Pallas kernels: 28 us -> 27 us
    pallas_call x1, Pallas kernels: 28 us -> 27 us  [layer(): pl.pallas_call(kernel, out_shape=jax.ShapeDtypeStruct((tokens, channels),...]
where the time goes in v2:
time: 28.8 us; the launch traced here: 28.7 us
  Pallas kernels  27 us (94%)
  local copies, waits for them, and re-layouts  1.67 us (6%)
    pallas_call x1, Pallas kernels, layer(): pl.pallas_call(kernel, out_shape=jax.ShapeDtypeStruct((tokens, channels),...  27 us
    unnamed x1, local copies, waits for them, and re-layouts  1.67 us

profile of v2, /device:TPU:6, one launch (start us, length us, event | category | flops | bytes accessed | tf_op | source)
XLA Modules:
  0.0 28.7 jit_solution(12048766015624074740)
XLA Ops:
  0.0 27.0 %layer.1 = bf16[512,256]{1,0:T(8,128)(2,1)} custom-call(bf16[512,256]{1,0:T(8,128)(2,1)} %q_hbm.1, bf16[512,256]{1,0:T(8,128)(2,1)} %k_hbm.1, bf16[512,256]{1,0:T(8,128)(2,1)} %v_hbm.1, f32[16,256]{1,0:T(8,128)} %decay_hbm.1, f32[16,256]{1,0:T(8,128)} %residue_hbm.1, f32[1,256]{1,0:T(1,128)} %bitcast.2, bf16[1024,256]{1,0:T(8,128)(2,1)} %w_hbm.1, ...), custom_call_target="tpu_custom_call" | custom-call | tf_op jit(solution)/shard_map/layer/pallas_call | solution.py:537
  27.0 1.7 %copy.10 = bf16[512,256]{1,0:T(8,128)(2,1)} copy(bf16[512,256]{1,0:T(8,128)(2,1)} %layer.1) | data formatting | bytes 524288

commit v3 on v2

--- a/solution.py
+++ b/solution.py
@@ -189,6 +189,8 @@
     decay = decay_ref[...]
     lam_buf[y] = jnp.exp(-decay)
 
+    scan_power = {shift: jnp.exp(-decay * float(steps * shift)) for shift in (1, 2, 4)}
+
     loads[0].wait()
     loads[1].wait()
     for lane in lane_starts:
@@ -208,7 +210,7 @@
         for n in range(modes):
             run = state[n]
             for shift in (1, 2, 4):
-                factor = jnp.exp(-rows_of(decay, n, lane) * float(steps * shift))
+                factor = rows_of(scan_power[shift], n, lane)
                 moved = jnp.where(sublane >= shift, pltpu.roll(run, shift, 0), 0.0)
                 run = run + factor * moved
             z_buf[pl.ds(z, 1), pl.ds(n, 1), pl.ds(lane, LANES)] = run[SUB - 1 : SUB].reshape(1, 1, LANES)
@@ -536,7 +538,7 @@
     ]
     return pl.pallas_call(
         kernel,
-        out_shape=jax.ShapeDtypeStruct((tokens, channels), BF16),
+        out_shape=pltpu.VMEM((tokens, channels), BF16),
         in_specs=[any_spec] * 8,
         out_specs=pl.BlockSpec(memory_space=pltpu.VMEM),
         scratch_shapes=[pltpu.VMEM(*shape) for shape in shapes]

time: 28.8 us -> 27.2 us (0.944)
  local copies, waits for them, and re-layouts: 1.67 us -> 0.71 us
  Pallas kernels: 27 us -> 26.4 us
    unnamed x1, local copies, waits for them, and re-layouts: 1.67 us -> 0.71 us
    pallas_call x1, Pallas kernels: 27 us -> 26.4 us  [layer(): pl.pallas_call(kernel, out_shape=pltpu.VMEM((tokens, channels), BF16), in...]
where the time goes in v3:
time: 27.2 us; the launch traced here: 27.1 us
  Pallas kernels  26.4 us (97%)
  local copies, waits for them, and re-layouts  0.71 us (3%)
    pallas_call x1, Pallas kernels, layer(): pl.pallas_call(kernel, out_shape=pltpu.VMEM((tokens, channels), BF16), in...  26.4 us
    unnamed x1, local copies, waits for them, and re-layouts  0.71 us

profile of v3, /device:TPU:6, one launch (start us, length us, event | category | flops | bytes accessed | tf_op | source)
XLA Modules:
  0.0 27.1 jit_solution(10158365762194963152)
XLA Ops:
  0.0 26.4 %layer.1 = bf16[512,256]{1,0:T(8,128)(2,1)S(1)} custom-call(bf16[512,256]{1,0:T(8,128)(2,1)} %q_hbm.1, bf16[512,256]{1,0:T(8,128)(2,1)} %k_hbm.1, bf16[512,256]{1,0:T(8,128)(2,1)} %v_hbm.1, f32[16,256]{1,0:T(8,128)} %decay_hbm.1, f32[16,256]{1,0:T(8,128)} %residue_hbm.1, f32[1,256]{1,0:T(1,128)} %bitcast.2, bf16[1024,256]{1,0:T(8,128)(2,1)} %w_hbm.1, ...), custom_call_target="tpu_custom_call" | custom-call | tf_op jit(solution)/shard_map/layer/pallas_call | solution.py:539
  26.4 0.7 %copy.10 = bf16[512,256]{1,0:T(8,128)(2,1)} copy(bf16[512,256]{1,0:T(8,128)(2,1)S(1)} %layer.1) | data formatting | bytes 524288

commit v4 on v3

--- a/solution.py
+++ b/solution.py
@@ -276,15 +276,14 @@
                 h_buf[n, :, pl.ds(lane, LANES)] = last[n]
         if begin == 0:
             ring_start(1, 0)
+            for k in range(1, NZ):
+                @pl.when(lead & (z + k < NZ))
+                def _(k=k):
+                    send_forward(k)
 
     @pl.when(lead)
     def _():
         ring_start(1, 1)
-
-    for k in range(1, NZ):
-        @pl.when(lead & (z + k < NZ))
-        def _(k=k):
-            send_forward(k)
 
     @pl.when(lead)
     def _():
@@ -394,7 +393,7 @@
                 return state
 
             first = tuple(g_buf[n, :, pl.ds(lane, LANES)] for n in range(modes))
-            last = lax.fori_loop(begin // 2, end // 2, step, first, unroll=4)
+            last = lax.fori_loop(begin // 2, end // 2, step, first, unroll=2)
             for n in range(modes):
                 g_buf[n, :, pl.ds(lane, LANES)] = last[n]
 

time: 27.2 us -> 27.2 us (level)
  no operation moved by 1% of the time
where the time goes in v4:
time: 27.2 us; the launch traced here: 27.1 us
  Pallas kernels  26.4 us (97%)
  local copies, waits for them, and re-layouts  0.71 us (3%)
    pallas_call x1, Pallas kernels, layer(): pl.pallas_call(kernel, out_shape=pltpu.VMEM((tokens, channels), BF16), in...  26.4 us
    unnamed x1, local copies, waits for them, and re-layouts  0.71 us

profile of v4, /device:TPU:6, one launch (start us, length us, event | category | flops | bytes accessed | tf_op | source)
XLA Modules:
  0.0 27.1 jit_solution(11881553155949263431)
XLA Ops:
  0.0 26.4 %layer.1 = bf16[512,256]{1,0:T(8,128)(2,1)S(1)} custom-call(bf16[512,256]{1,0:T(8,128)(2,1)} %q_hbm.1, bf16[512,256]{1,0:T(8,128)(2,1)} %k_hbm.1, bf16[512,256]{1,0:T(8,128)(2,1)} %v_hbm.1, f32[16,256]{1,0:T(8,128)} %decay_hbm.1, f32[16,256]{1,0:T(8,128)} %residue_hbm.1, f32[1,256]{1,0:T(1,128)} %bitcast.2, bf16[1024,256]{1,0:T(8,128)(2,1)} %w_hbm.1, ...), custom_call_target="tpu_custom_call" | custom-call | tf_op jit(solution)/shard_map/layer/pallas_call | solution.py:538
  26.4 0.7 %copy.10 = bf16[512,256]{1,0:T(8,128)(2,1)} copy(bf16[512,256]{1,0:T(8,128)(2,1)S(1)} %layer.1) | data formatting | bytes 524288
